TPU v7x, 256 devices: a whole 4x4x8 slice. The times are simulated.
256 devices in a mesh: leaf: 16 (over x, y), row: 16 (over z, core).
Axes of the slice: x: 4, y: 4, z: 8, core: 2. Of those that a mesh axis runs over, the one named last changes fastest.
Arguments:
- rhs: bfloat16 [6, 16, 512, 256], P(None, 'leaf', 'row'), may hold values from -6 to 6
- diag_inverse: bfloat16 [16, 6, 512, 512], P('leaf'), as said below
- factor: bfloat16 [16, 178, 512, 512], P('leaf', None, 'row'), as said below
- widths: int32 [6, 16], P(None, 'leaf'), may hold values from 64 to 512, as said below
- structure: int32 [16, 178], P('leaf'), may hold values from 0 to 1, as said below
Outputs:
- forward_solution: bfloat16 [6, 16, 512, 256], P(None, 'leaf', 'row')
- adjoint_solution: bfloat16 [6, 16, 512, 256], P(None, 'leaf', 'row')
Inputs may be any that keep to these rules, and one draw needn't show every extreme that they name: `widths`: every draw has a supernode of exactly 512 columns and one of exactly one eighth of 512 columns. `structure`: 1 where the block is present. Each diag_inverse[j, l] is lower triangular with diagonal entries from 0.5 to 1. `factor`: dense blocks of independent entries.
All inputs are finite; a program needn't handle non-finite values.
Results may differ from a plain program's by a relative error of at most 0.017.
Values may be sent and summed in bfloat16 or wider, within the bound.
A program may use at most 64 MiB of HBM per device.

v0:
```python
import jax
import jax.numpy as jnp
from jax import lax
from jax.sharding import PartitionSpec as P


def group_size(level_now, leaf_count):
    return min(2**level_now, leaf_count)


def block_offsets(levels, leaf_count):
    offset_table = {}
    cursor = 0
    for source_level in range(levels):
        for target_level in range(source_level + 1, levels):
            offset_table[source_level, target_level] = cursor
            cursor += group_size(target_level, leaf_count)
    return offset_table


def blocks_after(level_now, levels, leaf_count):
    return sum(
        (group_size(target_level, leaf_count) for target_level in range(level_now + 1, levels))
    )


def contract_rows(left_side, right_side):
    return lax.dot_general(
        left_side, right_side, (((0,), (0,)), ((), ())), preferred_element_type=jnp.float32
    )


def apply_columns(matrix, shard_piece):
    return jnp.dot(matrix, shard_piece, preferred_element_type=jnp.float32)


def group_reduce(partials, group_span, leaf_count, leaf_index):
    group_base = leaf_index // group_span * group_span
    spread = jnp.zeros((leaf_count,) + partials.shape[1:], jnp.float32)
    spread = lax.dynamic_update_slice_in_dim(spread, partials, group_base, 0)
    return lax.psum_scatter(
        spread.astype(jnp.bfloat16), "leaf", scatter_dimension=0, tiled=True
    ).astype(jnp.float32)[0]


def group_collect(own_block, group_span, leaf_index):
    everyone = lax.all_gather(own_block[None], "leaf", axis=0, tiled=True)
    group_base = leaf_index // group_span * group_span
    return lax.dynamic_slice_in_dim(everyone, group_base, group_span, 0)


def adjoint_level(flat_blocks, flat_values, own_full, full_mask, block_mask, inverse_cols):
    pulled = lax.psum(contract_rows(flat_blocks, flat_values).astype(jnp.bfloat16), "row").astype(
        jnp.float32
    )
    reduced_full = (full_mask[:, None] * (own_full.astype(jnp.float32) - pulled)).astype(
        jnp.bfloat16
    )
    solved = contract_rows(inverse_cols, reduced_full)
    return (block_mask[:, None] * solved).astype(jnp.bfloat16)


def shards(rhs, diag_inverse, factor, widths, structure):
    leaf_count = lax.axis_size("leaf")
    leaf_index = lax.axis_index("leaf")
    row_index = lax.axis_index("row")
    levels = rhs.shape[0]
    block_rows = rhs.shape[2]
    columns = rhs.shape[3]
    full_width = factor.shape[3]
    inverse = diag_inverse[0]
    blocks = factor[0]
    weights = structure[0].astype(jnp.float32)
    own_rows = row_index * block_rows
    positions = jnp.arange(full_width, dtype=jnp.int32)
    full_masks = (positions[None, :] < widths).astype(jnp.float32)
    block_masks = lax.dynamic_slice_in_dim(full_masks, own_rows, block_rows, 1)
    offset_table = block_offsets(levels, leaf_count)
    pending = {}
    for target_level in range(1, levels):
        pending[target_level] = jnp.zeros(
            (group_size(target_level, leaf_count), block_rows, columns), jnp.float32
        )
    forward_blocks = []
    forward_full = []
    for level_now in range(levels):
        if level_now > 0:
            incoming = group_reduce(
                pending[level_now], group_size(level_now, leaf_count), leaf_count, leaf_index
            )
        else:
            incoming = jnp.zeros((block_rows, columns), jnp.float32)
        residual = (
            block_masks[level_now][:, None] * (rhs[level_now, 0].astype(jnp.float32) - incoming)
        ).astype(jnp.bfloat16)
        solve_rows = inverse[level_now]
        folded = apply_columns(solve_rows, lax.all_gather(residual, "row", axis=0, tiled=True))
        solved_full = (full_masks[level_now][:, None] * folded).astype(jnp.bfloat16)
        solved_block = lax.dynamic_slice_in_dim(solved_full, own_rows, block_rows, 0)
        forward_blocks.append(solved_block)
        forward_full.append(solved_full)
        if level_now + 1 < levels:
            first_block = offset_table[level_now, level_now + 1]
            block_count = blocks_after(level_now, levels, leaf_count)
            chosen = blocks[first_block : first_block + block_count].reshape(
                block_count * block_rows, full_width
            )
            products = jnp.dot(chosen, solved_full, preferred_element_type=jnp.float32).reshape(
                block_count, block_rows, columns
            )
            products = products * weights[first_block : first_block + block_count][:, None, None]
            cursor = 0
            for target_level in range(level_now + 1, levels):
                group_span = group_size(target_level, leaf_count)
                pending[target_level] = (
                    pending[target_level] + products[cursor : cursor + group_span]
                )
                cursor += group_span
    gathered = {}
    adjoint_blocks = [None] * levels
    for level_now in reversed(range(levels)):
        inverse_cols = lax.dynamic_slice_in_dim(inverse[level_now], own_rows, block_rows, 1)
        if level_now + 1 == levels:
            solved = contract_rows(inverse_cols, forward_full[level_now])
            own_adjoint = (block_masks[level_now][:, None] * solved).astype(jnp.bfloat16)
        else:
            first_block = offset_table[level_now, level_now + 1]
            block_count = blocks_after(level_now, levels, leaf_count)
            stacked = jnp.concatenate(
                [gathered[upper_level] for upper_level in range(level_now + 1, levels)], 0
            )
            stacked = stacked * structure[0, first_block : first_block + block_count][
                :, None, None
            ].astype(jnp.bfloat16)
            flat_blocks = blocks[first_block : first_block + block_count].reshape(
                block_count * block_rows, full_width
            )
            flat_values = stacked.reshape(block_count * block_rows, columns)
            own_adjoint = adjoint_level(
                flat_blocks,
                flat_values,
                forward_full[level_now],
                full_masks[level_now],
                block_masks[level_now],
                inverse_cols,
            )
        adjoint_blocks[level_now] = own_adjoint
        if level_now > 0:
            gathered[level_now] = group_collect(
                own_adjoint, group_size(level_now, leaf_count), leaf_index
            )
    return (jnp.stack(forward_blocks)[:, None], jnp.stack(adjoint_blocks)[:, None])


def solution(mesh):
    placed = (
        P(None, "leaf", "row", None),
        P("leaf", None, None, None),
        P("leaf", None, "row", None),
        P(None, "leaf"),
        P("leaf", None),
    )
    return jax.shard_map(
        shards,
        mesh=mesh,
        in_specs=placed,
        out_specs=(P(None, "leaf", "row", None), P(None, "leaf", "row", None)),
        check_vma=False,
    )
```

profile of v0, /device:TPU:1, one launch (start us, length us, event | category | flops | bytes accessed | tf_op | source)
XLA Modules:
  0.0 1223.9 jit_solution(11152830773635222627)
XLA Ops:
  8.9 22.0 %all_gather.33 = bf16[512,256]{1,0:T(8,128)(2,1)S(1)} all-gather(bf16[32,256]{1,0:T(8,128)(2,1)S(1)} %fusion.72), channel_id=1, replica_groups=mesh['leaf'=16,'row'=16] {'row'}, dimensions={0}, use_global_device_ids=true | all-gather | bytes 278528 | tf_op jit(solution)/shard_map/all_gather | solution.py:97
  38.4 71.6 %reduce-scatter.16.cloned.1.call-done = bf16[1,32,256]{2,1,0:T(8,128)(2,1)} async-done(((bf16[16,32,256]{2,1,0:T(8,128)(2,1)}), bf16[1,32,256]{2,1,0:T(8,128)(2,1)}) %reduce-scatter.16.cloned.1.call-update) | async-done | bytes 16400
  110.8 20.2 %all_gather.34 = bf16[512,256]{1,0:T(8,128)(2,1)S(1)} all-gather(bf16[32,256]{1,0:T(8,128)(2,1)S(1)} %fusion.71), channel_id=1, replica_groups=mesh['leaf'=16,'row'=16] {'row'}, dimensions={0}, use_global_device_ids=true | all-gather | bytes 278528 | tf_op jit(solution)/shard_map/all_gather | solution.py:97
  133.1 1.7 convolution_bitcast_fusion.1
  134.8 2.9 copy.19
  142.1 2.5 slice.238
  144.7 69.2 %reduce-scatter.18.cloned.1.call-done = bf16[1,32,256]{2,1,0:T(8,128)(2,1)} async-done(((bf16[16,32,256]{2,1,0:T(8,128)(2,1)}), bf16[1,32,256]{2,1,0:T(8,128)(2,1)}) %reduce-scatter.18.cloned.1.call-update) | async-done | bytes 16400
  214.8 20.3 %all_gather.35 = bf16[512,256]{1,0:T(8,128)(2,1)S(1)} all-gather(bf16[32,256]{1,0:T(8,128)(2,1)S(1)} %fusion.69), channel_id=1, replica_groups=mesh['leaf'=16,'row'=16] {'row'}, dimensions={0}, use_global_device_ids=true | all-gather | bytes 278528 | tf_op jit(solution)/shard_map/all_gather | solution.py:97
  237.2 1.6 convolution_bitcast_fusion
  238.8 2.8 copy.20
  246.0 2.3 slice.249
  248.5 69.3 %reduce-scatter.20.cloned.1.call-done = bf16[1,32,256]{2,1,0:T(8,128)(2,1)} async-done(((bf16[16,32,256]{2,1,0:T(8,128)(2,1)}), bf16[1,32,256]{2,1,0:T(8,128)(2,1)}) %reduce-scatter.20.cloned.1.call-update) | async-done | bytes 16400
  318.6 20.2 %all_gather.36 = bf16[512,256]{1,0:T(8,128)(2,1)S(1)} all-gather(bf16[32,256]{1,0:T(8,128)(2,1)S(1)} %fusion.67), channel_id=1, replica_groups=mesh['leaf'=16,'row'=16] {'row'}, dimensions={0}, use_global_device_ids=true | all-gather | bytes 278528 | tf_op jit(solution)/shard_map/all_gather | solution.py:97
  342.5 2.6 copy.21
  347.5 2.2 fusion.21
  352.1 69.4 %reduce-scatter.22.cloned.1.call-done = bf16[1,32,256]{2,1,0:T(8,128)(2,1)} async-done(((bf16[16,32,256]{2,1,0:T(8,128)(2,1)}), bf16[1,32,256]{2,1,0:T(8,128)(2,1)}) %reduce-scatter.22.cloned.1.call-update) | async-done | bytes 16400
  422.3 20.3 %all_gather.37 = bf16[512,256]{1,0:T(8,128)(2,1)S(1)} all-gather(bf16[32,256]{1,0:T(8,128)(2,1)S(1)} %fusion.65), channel_id=1, replica_groups=mesh['leaf'=16,'row'=16] {'row'}, dimensions={0}, use_global_device_ids=true | all-gather | bytes 278528 | tf_op jit(solution)/shard_map/all_gather | solution.py:97
  445.9 2.1 copy.22
  448.0 2.5 fusion.20
  451.1 3.5 fusion.86
  454.7 67.7 %reduce-scatter.24.cloned.1.call-done = bf16[1,32,256]{2,1,0:T(8,128)(2,1)} async-done(((bf16[16,32,256]{2,1,0:T(8,128)(2,1)}), bf16[1,32,256]{2,1,0:T(8,128)(2,1)}) %reduce-scatter.24.cloned.1.call-update) | async-done | bytes 16400
  523.2 20.2 %all_gather.38 = bf16[512,256]{1,0:T(8,128)(2,1)S(1)} all-gather(bf16[32,256]{1,0:T(8,128)(2,1)S(1)} %fusion.63), channel_id=1, replica_groups=mesh['leaf'=16,'row'=16] {'row'}, dimensions={0}, use_global_device_ids=true | all-gather | bytes 278528 | tf_op jit(solution)/shard_map/all_gather | solution.py:97
  546.1 18.0 %all-gather = bf16[512,256]{1,0:T(8,128)(2,1)S(1)} all-gather(bf16[32,256]{1,0:T(8,128)(2,1)S(1)} %fusion.11), channel_id=2, replica_groups=mesh['leaf'=16,'row'=16] {'leaf'}, dimensions={0}, use_global_device_ids=true | all-gather | bytes 278528 | tf_op jit(solution)/shard_map/all_gather | solution.py:47
  569.0 105.7 %all-reduce.11.cloned.1.call-done = bf16[512,256]{0,1:T(8,128)(2,1)} async-done(((bf16[512,256]{0,1:T(8,128)(2,1)}), bf16[512,256]{0,1:T(8,128)(2,1)}) %all-reduce.11.cloned.1.call-update) | async-done | bytes 262160 | tf_op jit(solution)/shard_map/psum | solution.py:53
  676.1 18.5 %all-gather.1 = bf16[512,256]{1,0:T(8,128)(2,1)S(1)} all-gather(bf16[32,256]{1,0:T(8,128)(2,1)S(1)} %fusion.12), channel_id=3, replica_groups=mesh['leaf'=16,'row'=16] {'leaf'}, dimensions={0}, use_global_device_ids=true | all-gather | bytes 278528 | tf_op jit(solution)/shard_map/all_gather | solution.py:47
  699.9 109.0 %all-reduce.13.cloned.1.call-done = bf16[512,256]{0,1:T(8,128)(2,1)} async-done(((bf16[512,256]{0,1:T(8,128)(2,1)}), bf16[512,256]{0,1:T(8,128)(2,1)}) %all-reduce.13.cloned.1.call-update) | async-done | bytes 262160 | tf_op jit(solution)/shard_map/psum | solution.py:53
  810.4 18.5 %all-gather.2 = bf16[512,256]{1,0:T(8,128)(2,1)S(1)} all-gather(bf16[32,256]{1,0:T(8,128)(2,1)S(1)} %fusion.13), channel_id=4, replica_groups=mesh['leaf'=16,'row'=16] {'leaf'}, dimensions={0}, use_global_device_ids=true | all-gather | bytes 278528 | tf_op jit(solution)/shard_map/all_gather | solution.py:47
  837.5 107.2 %all-reduce.15.cloned.1.call-done = bf16[512,256]{0,1:T(8,128)(2,1)} async-done(((bf16[512,256]{0,1:T(8,128)(2,1)}), bf16[512,256]{0,1:T(8,128)(2,1)}) %all-reduce.15.cloned.1.call-update) | async-done | bytes 262160 | tf_op jit(solution)/shard_map/psum | solution.py:53
  946.1 18.7 %all-gather.3 = bf16[512,256]{1,0:T(8,128)(2,1)S(1)} all-gather(bf16[32,256]{1,0:T(8,128)(2,1)S(1)} %fusion.14), channel_id=5, replica_groups=mesh['leaf'=16,'row'=16] {'leaf'}, dimensions={0}, use_global_device_ids=true | all-gather | bytes 278528 | tf_op jit(solution)/shard_map/all_gather | solution.py:47
  969.6 110.7 %all-reduce.17.cloned.1.call-done = bf16[512,256]{0,1:T(8,128)(2,1)} async-done(((bf16[512,256]{0,1:T(8,128)(2,1)}), bf16[512,256]{0,1:T(8,128)(2,1)}) %all-reduce.17.cloned.1.call-update) | async-done | bytes 262160 | tf_op jit(solution)/shard_map/psum | solution.py:53
  1081.7 18.5 %all-gather.4 = bf16[512,256]{1,0:T(8,128)(2,1)S(1)} all-gather(bf16[32,256]{1,0:T(8,128)(2,1)S(1)} %fusion.15), channel_id=6, replica_groups=mesh['leaf'=16,'row'=16] {'leaf'}, dimensions={0}, use_global_device_ids=true | all-gather | bytes 278528 | tf_op jit(solution)/shard_map/all_gather | solution.py:47
  1103.9 111.1 %all-reduce.19.cloned.1.call-done = bf16[512,256]{0,1:T(8,128)(2,1)} async-done(((bf16[512,256]{0,1:T(8,128)(2,1)}), bf16[512,256]{0,1:T(8,128)(2,1)}) %all-reduce.19.cloned.1.call-update) | async-done | bytes 262160 | tf_op jit(solution)/shard_map/psum | solution.py:53
  (202 shorter events, 75.7 us)
Async XLA Ops:
  7.2 102.8 %reduce-scatter.16.cloned.1.call-start = ((), (), s32[]{:S(2)}) async-start(), calls=%async_computation.10 | async-start | bytes 278528
  8.0 24.6 %copy-start.31 = (f32[1,512]{1,0:T(1,128)}, f32[1,512]{1,0:T(1,128)S(1)}, u32[]{:S(2)}) copy-start(f32[1,512]{1,0:T(1,128)S(1)} %get-tuple-element.19) | copy-start | bytes 6148
  8.0 123.0 %copy-start.33 = (f32[1,512]{1,0:T(1,128)}, f32[1,512]{1,0:T(1,128)S(1)}, u32[]{:S(2)}) copy-start(f32[1,512]{1,0:T(1,128)S(1)} %get-tuple-element.18) | copy-start | bytes 6148
  8.0 227.1 %copy-start.35 = (f32[1,512]{1,0:T(1,128)}, f32[1,512]{1,0:T(1,128)S(1)}, u32[]{:S(2)}) copy-start(f32[1,512]{1,0:T(1,128)S(1)} %get-tuple-element.17) | copy-start | bytes 6148
  8.0 330.9 %copy-start.36 = (f32[1,512]{1,0:T(1,128)}, f32[1,512]{1,0:T(1,128)S(1)}, u32[]{:S(2)}) copy-start(f32[1,512]{1,0:T(1,128)S(1)} %get-tuple-element.16) | copy-start | bytes 6148
  8.0 434.6 %copy-start.37 = (f32[1,512]{1,0:T(1,128)}, f32[1,512]{1,0:T(1,128)S(1)}, u32[]{:S(2)}) copy-start(f32[1,512]{1,0:T(1,128)S(1)} %get-tuple-element.15) | copy-start | bytes 6148
  8.1 101.9 %copy-start.40 = (f32[32]{0:T(128)}, f32[32]{0:T(128)S(1)}, u32[]{:S(2)}) copy-start(f32[32]{0:T(128)S(1)} %get-tuple-element.24) | copy-start | bytes 388
  8.1 205.8 %copy-start.42 = (f32[32]{0:T(128)}, f32[32]{0:T(128)S(1)}, u32[]{:S(2)}) copy-start(f32[32]{0:T(128)S(1)} %get-tuple-element.23) | copy-start | bytes 388
  8.1 309.6 %copy-start.43 = (f32[32]{0:T(128)}, f32[32]{0:T(128)S(1)}, u32[]{:S(2)}) copy-start(f32[32]{0:T(128)S(1)} %get-tuple-element.22) | copy-start | bytes 388
  8.1 413.4 %copy-start.44 = (f32[32]{0:T(128)}, f32[32]{0:T(128)S(1)}, u32[]{:S(2)}) copy-start(f32[32]{0:T(128)S(1)} %get-tuple-element.21) | copy-start | bytes 388
  36.7 73.2 %copy-start.29 = (bf16[6,1,32,256]{3,2,1,0:T(8,128)(2,1)S(1)}, bf16[6,1,32,256]{3,2,1,0:T(8,128)(2,1)}, u32[]{:S(2)}) copy-start(bf16[6,1,32,256]{3,2,1,0:T(8,128)(2,1)} %param.5) | copy-start | bytes 294916
  36.7 177.2 %reduce-scatter.18.cloned.1.call-start = ((), (), s32[]{:S(2)}) async-start(), calls=%async_computation.11 | async-start | bytes 278528
  142.0 175.7 %reduce-scatter.20.cloned.1.call-start = ((), (), s32[]{:S(2)}) async-start(), calls=%async_computation.12 | async-start | bytes 278528
  245.9 175.6 %reduce-scatter.22.cloned.1.call-start = ((), (), s32[]{:S(2)}) async-start(), calls=%async_computation.13 | async-start | bytes 278528
  349.7 172.6 %reduce-scatter.24.cloned.1.call-start = ((), (), s32[]{:S(2)}) async-start(), calls=%async_computation.14 | async-start | bytes 278528
  350.9 95.0 %copy-start.5 = (bf16[1,16,32,512]{3,2,1,0:T(8,128)(2,1)}, bf16[1,16,32,512]{3,2,1,0:T(8,128)(2,1)S(1)}, u32[]{:S(2)}) copy-start(bf16[1,16,32,512]{3,2,1,0:T(8,128)(2,1)S(1)} %slice.261) | copy-start | bytes 1572868
  450.5 224.2 %all-reduce.11.cloned.1.call-start = ((), (), s32[]{:S(2)}) async-start(), calls=%async_computation.5 | async-start | bytes 524288 | tf_op jit(solution)/shard_map/psum | solution.py:53
  522.3 41.9 %copy-start.6 = (bf16[1,16,32,512]{3,2,1,0:T(8,128)(2,1)S(1)}, bf16[1,16,32,512]{3,2,1,0:T(8,128)(2,1)}, u32[]{:S(2)}) copy-start(bf16[1,16,32,512]{3,2,1,0:T(8,128)(2,1)} %copy-done.5) | copy-start | bytes 1572868
  544.8 129.9 %copy-start.14 = (bf16[256,512]{1,0:T(8,128)(2,1)S(1)}, bf16[256,512]{1,0:T(8,128)(2,1)}, u32[]{:S(2)}) copy-start(bf16[256,512]{1,0:T(8,128)(2,1)} %copy-done.13) | copy-start | bytes 786436
  565.2 243.7 %all-reduce.13.cloned.1.call-start = ((), (), s32[]{:S(2)}) async-start(), calls=%async_computation.6 | async-start | bytes 524288 | tf_op jit(solution)/shard_map/psum | solution.py:53
  696.5 248.2 %all-reduce.15.cloned.1.call-start = ((), (), s32[]{:S(2)}) async-start(), calls=%async_computation.7 | async-start | bytes 524288 | tf_op jit(solution)/shard_map/psum | solution.py:53
  832.3 248.0 %all-reduce.17.cloned.1.call-start = ((), (), s32[]{:S(2)}) async-start(), calls=%async_computation.8 | async-start | bytes 524288 | tf_op jit(solution)/shard_map/psum | solution.py:53
  966.5 113.7 %copy-start.34 = (f32[1,512]{1,0:T(1,128)S(1)}, f32[1,512]{1,0:T(1,128)}, u32[]{:S(2)}) copy-start(f32[1,512]{1,0:T(1,128)} %copy-done.33) | copy-start | bytes 6148
  966.5 113.7 %copy-start.41 = (f32[32]{0:T(128)S(1)}, f32[32]{0:T(128)}, u32[]{:S(2)}) copy-start(f32[32]{0:T(128)} %copy-done.40) | copy-start | bytes 388
  967.8 133.2 %copy-start.19 = (bf16[512,256]{1,0:T(8,128)(2,1)S(1)}, bf16[512,256]{1,0:T(8,128)(2,1)}, u32[]{:S(2)}) copy-start(bf16[512,256]{1,0:T(8,128)(2,1)} %copy-done.18) | copy-start | bytes 786436
  967.9 133.2 %copy-start.47 = (bf16[46]{0:T(256)(128)(2,1)S(1)}, bf16[46]{0:T(256)(128)(2,1)}, u32[]{:S(2)}) copy-start(bf16[46]{0:T(256)(128)(2,1)} %slice_bitcast_fusion) | copy-start | bytes 280
  967.9 247.1 %all-reduce.19.cloned.1.call-start = ((), (), s32[]{:S(2)}) async-start(), calls=%async_computation.9 | async-start | bytes 524288 | tf_op jit(solution)/shard_map/psum | solution.py:53
  1101.2 113.8 %copy-start.11 = (bf16[256,512]{1,0:T(8,128)(2,1)S(1)}, bf16[256,512]{1,0:T(8,128)(2,1)}, u32[]{:S(2)}) copy-start(bf16[256,512]{1,0:T(8,128)(2,1)} %copy-done.10) | copy-start | bytes 786436
  1101.2 113.8 %copy-start.32 = (f32[1,512]{1,0:T(1,128)S(1)}, f32[1,512]{1,0:T(1,128)}, u32[]{:S(2)}) copy-start(f32[1,512]{1,0:T(1,128)} %copy-done.31) | copy-start | bytes 6148
  1101.3 113.8 %copy-start.39 = (f32[32]{0:T(128)S(1)}, f32[32]{0:T(128)}, u32[]{:S(2)}) copy-start(f32[32]{0:T(128)} %copy-done.38) | copy-start | bytes 388
  1101.3 115.1 %copy-start.28 = (bf16[32,256]{1,0:T(8,128)(2,1)S(1)}, bf16[32,256]{1,0:T(8,128)(2,1)}, u32[]{:S(2)}) copy-start(bf16[32,256]{1,0:T(8,128)(2,1)} %copy-done.27) | copy-start | bytes 49156
  1101.3 115.1 %copy-start.26 = (bf16[32,256]{1,0:T(8,128)(2,1)S(1)}, bf16[32,256]{1,0:T(8,128)(2,1)}, u32[]{:S(2)}) copy-start(bf16[32,256]{1,0:T(8,128)(2,1)} %copy-done.25) | copy-start | bytes 49156
  (26 other events, 165.3 us)
Sparse Core Ops, SparseCore 0:
  36.8 73.0 reduce-scatter.15
  142.2 71.6 reduce-scatter.17
  246.1 71.6 reduce-scatter.19
  349.8 71.6 reduce-scatter.21
  450.6 71.6 reduce-scatter.23
  565.4 109.3 all-reduce.10
  696.6 112.2 all-reduce.12
  832.4 112.2 all-reduce.14
  968.0 112.2 all-reduce.16
  1102.7 112.2 all-reduce.18
where the time goes:
time: 1230 us; the launch traced here: 1220 us
  waiting for transfers between devices  891 us (72%)
  blocking collectives  215 us (17%)
  local copies, waits for them, and re-layouts  53.4 us (4%)
  matrix products  29 us (2%)
  other arithmetic  19.6 us (2%)
  between operations  15 us (1%)
    psum x5, waiting for transfers between devices, adjoint_level(): lax.psum(contract_rows(flat_blocks, flat_values).astype(jnp.bfloat16), 'r...  544 us
    unnamed x15, waiting for transfers between devices  347 us
    all_gather x6, blocking collectives, shards(): lax.all_gather(residual, 'row', axis=0, tiled=True)  123 us
    all_gather x5, blocking collectives, group_collect(): everyone = lax.all_gather(own_block[None], 'leaf', axis=0, tiled=True)  92.2 us
  transfers between devices with their start and end apart: 10, of which 10 were waited for; matrix products, arithmetic and copies ran while one was open for 2% of the time, Pallas kernels for 0%

commit v1 on v0

--- a/solution.py
+++ b/solution.py
@@ -50,9 +50,9 @@
 
 
 def adjoint_level(flat_blocks, flat_values, own_full, full_mask, block_mask, inverse_cols):
-    pulled = lax.psum(contract_rows(flat_blocks, flat_values).astype(jnp.bfloat16), "row").astype(
-        jnp.float32
-    )
+    pulled = jnp.sum(
+        lax.all_gather(contract_rows(flat_blocks, flat_values).astype(jnp.bfloat16), "row"), axis=0
+    ).astype(jnp.float32)
     reduced_full = (full_mask[:, None] * (own_full.astype(jnp.float32) - pulled)).astype(
         jnp.bfloat16
     )

time: 1230 us -> 923 us (0.75)
  waiting for transfers between devices: 891 us -> 565 us
    psum x5 -> x0, waiting for transfers between devices: 544 us -> none  [adjoint_level(): lax.psum(contract_rows(flat_blocks, flat_values).astype(jnp.bfloat16), 'r...]
    all_gather x0 -> x5, waiting for transfers between devices: none -> 216 us  [adjoint_level(): lax.all_gather(contract_rows(flat_blocks, flat_values).astype(jnp.bfloat1...]
    unnamed x109 -> x104, local copies, waits for them, and re-layouts: 18.2 us -> 33.2 us
    reduce_sum x0 -> x5, other arithmetic: none -> 12.7 us  [adjoint_level(): jnp.sum(lax.all_gather(contract_rows(flat_blocks, flat_values).astype(jnp...]
where the time goes in v1:
time: 923 us; the launch traced here: 915 us
  waiting for transfers between devices  565 us (61%)
  blocking collectives  216 us (23%)
  local copies, waits for them, and re-layouts  59.9 us (6%)
  other arithmetic  30.2 us (3%)
  matrix products  27.2 us (3%)
  between operations  15.3 us (2%)
    unnamed x15, waiting for transfers between devices  349 us
    all_gather x5, waiting for transfers between devices, adjoint_level(): lax.all_gather(contract_rows(flat_blocks, flat_values).astype(jnp.bfloat1...  216 us
    all_gather x6, blocking collectives, shards(): lax.all_gather(residual, 'row', axis=0, tiled=True)  123 us
    all_gather x5, blocking collectives, group_collect(): everyone = lax.all_gather(own_block[None], 'leaf', axis=0, tiled=True)  92.4 us
    unnamed x104, local copies, waits for them, and re-layouts  33.2 us
  transfers between devices with their start and end apart: 10, of which 10 were waited for; matrix products, arithmetic and copies ran while one was open for 2% of the time, Pallas kernels for 0%

profile of v1, /device:TPU:1, one launch (start us, length us, event | category | flops | bytes accessed | tf_op | source)
XLA Modules:
  0.0 914.6 jit_solution(9649019794852929918)
XLA Ops:
  8.9 22.0 %all_gather.63 = bf16[512,256]{1,0:T(8,128)(2,1)S(1)} all-gather(bf16[32,256]{1,0:T(8,128)(2,1)S(1)} %fusion.72), channel_id=1, replica_groups=mesh['leaf'=16,'row'=16] {'row'}, dimensions={0}, use_global_device_ids=true | all-gather | bytes 278528 | tf_op jit(solution)/shard_map/all_gather | solution.py:97
  38.3 71.6 %reduce-scatter.16.cloned.1.call-done = bf16[1,32,256]{2,1,0:T(8,128)(2,1)} async-done(((bf16[16,32,256]{2,1,0:T(8,128)(2,1)}), bf16[1,32,256]{2,1,0:T(8,128)(2,1)}) %reduce-scatter.16.cloned.1.call-update) | async-done | bytes 16400
  110.7 20.2 %all_gather.64 = bf16[512,256]{1,0:T(8,128)(2,1)S(1)} all-gather(bf16[32,256]{1,0:T(8,128)(2,1)S(1)} %fusion.71), channel_id=1, replica_groups=mesh['leaf'=16,'row'=16] {'row'}, dimensions={0}, use_global_device_ids=true | all-gather | bytes 278528 | tf_op jit(solution)/shard_map/all_gather | solution.py:97
  134.7 2.9 copy.19
  142.0 2.5 slice.238
  144.6 69.2 %reduce-scatter.18.cloned.1.call-done = bf16[1,32,256]{2,1,0:T(8,128)(2,1)} async-done(((bf16[16,32,256]{2,1,0:T(8,128)(2,1)}), bf16[1,32,256]{2,1,0:T(8,128)(2,1)}) %reduce-scatter.18.cloned.1.call-update) | async-done | bytes 16400
  214.7 20.2 %all_gather.65 = bf16[512,256]{1,0:T(8,128)(2,1)S(1)} all-gather(bf16[32,256]{1,0:T(8,128)(2,1)S(1)} %fusion.69), channel_id=1, replica_groups=mesh['leaf'=16,'row'=16] {'row'}, dimensions={0}, use_global_device_ids=true | all-gather | bytes 278528 | tf_op jit(solution)/shard_map/all_gather | solution.py:97
  238.8 2.8 copy.20
  248.5 69.4 %reduce-scatter.20.cloned.1.call-done = bf16[1,32,256]{2,1,0:T(8,128)(2,1)} async-done(((bf16[16,32,256]{2,1,0:T(8,128)(2,1)}), bf16[1,32,256]{2,1,0:T(8,128)(2,1)}) %reduce-scatter.20.cloned.1.call-update) | async-done | bytes 16400
  318.7 20.2 %all_gather.66 = bf16[512,256]{1,0:T(8,128)(2,1)S(1)} all-gather(bf16[32,256]{1,0:T(8,128)(2,1)S(1)} %fusion.67), channel_id=1, replica_groups=mesh['leaf'=16,'row'=16] {'row'}, dimensions={0}, use_global_device_ids=true | all-gather | bytes 278528 | tf_op jit(solution)/shard_map/all_gather | solution.py:97
  342.6 2.6 copy.21
  350.9 70.6 %reduce-scatter.22.cloned.1.call-done = bf16[1,32,256]{2,1,0:T(8,128)(2,1)} async-done(((bf16[16,32,256]{2,1,0:T(8,128)(2,1)}), bf16[1,32,256]{2,1,0:T(8,128)(2,1)}) %reduce-scatter.22.cloned.1.call-update) | async-done | bytes 16400
  422.4 20.3 %all_gather.67 = bf16[512,256]{1,0:T(8,128)(2,1)S(1)} all-gather(bf16[32,256]{1,0:T(8,128)(2,1)S(1)} %fusion.65), channel_id=1, replica_groups=mesh['leaf'=16,'row'=16] {'row'}, dimensions={0}, use_global_device_ids=true | all-gather | bytes 278528 | tf_op jit(solution)/shard_map/all_gather | solution.py:97
  450.6 3.4 fusion.86
  454.0 68.3 %reduce-scatter.24.cloned.1.call-done = bf16[1,32,256]{2,1,0:T(8,128)(2,1)} async-done(((bf16[16,32,256]{2,1,0:T(8,128)(2,1)}), bf16[1,32,256]{2,1,0:T(8,128)(2,1)}) %reduce-scatter.24.cloned.1.call-update) | async-done | bytes 16400
  523.2 20.2 %all_gather.68 = bf16[512,256]{1,0:T(8,128)(2,1)S(1)} all-gather(bf16[32,256]{1,0:T(8,128)(2,1)S(1)} %fusion.63), channel_id=1, replica_groups=mesh['leaf'=16,'row'=16] {'row'}, dimensions={0}, use_global_device_ids=true | all-gather | bytes 278528 | tf_op jit(solution)/shard_map/all_gather | solution.py:97
  545.1 18.0 %all-gather = bf16[512,256]{1,0:T(8,128)(2,1)S(1)} all-gather(bf16[32,256]{1,0:T(8,128)(2,1)S(1)} %fusion.11), channel_id=2, replica_groups=mesh['leaf'=16,'row'=16] {'leaf'}, dimensions={0}, use_global_device_ids=true | all-gather | bytes 278528 | tf_op jit(solution)/shard_map/all_gather | solution.py:47
  564.8 42.9 %all-gather.16.cloned.1.call-done = bf16[8192,256]{0,1:T(8,128)(2,1)} async-done(((bf16[512,256]{0,1:T(8,128)(2,1)}), bf16[8192,256]{0,1:T(8,128)(2,1)}) %all-gather.16.cloned.1.call-update) | async-done | bytes 4194320 | tf_op jit(solution)/shard_map/all_gather | solution.py:54
  607.7 4.0 copy.31
  615.6 18.6 %all-gather.2 = bf16[512,256]{1,0:T(8,128)(2,1)S(1)} all-gather(bf16[32,256]{1,0:T(8,128)(2,1)S(1)} %fusion.12), channel_id=4, replica_groups=mesh['leaf'=16,'row'=16] {'leaf'}, dimensions={0}, use_global_device_ids=true | all-gather | bytes 278528 | tf_op jit(solution)/shard_map/all_gather | solution.py:47
  635.6 44.1 %all-gather.18.cloned.1.call-done = bf16[8192,256]{0,1:T(8,128)(2,1)} async-done(((bf16[512,256]{0,1:T(8,128)(2,1)}), bf16[8192,256]{0,1:T(8,128)(2,1)}) %all-gather.18.cloned.1.call-update) | async-done | bytes 4194320 | tf_op jit(solution)/shard_map/all_gather | solution.py:54
  679.7 4.0 copy.32
  687.6 18.6 %all-gather.4 = bf16[512,256]{1,0:T(8,128)(2,1)S(1)} all-gather(bf16[32,256]{1,0:T(8,128)(2,1)S(1)} %fusion.13), channel_id=6, replica_groups=mesh['leaf'=16,'row'=16] {'leaf'}, dimensions={0}, use_global_device_ids=true | all-gather | bytes 278528 | tf_op jit(solution)/shard_map/all_gather | solution.py:47
  709.8 43.4 %all-gather.20.cloned.1.call-done = bf16[8192,256]{0,1:T(8,128)(2,1)} async-done(((bf16[512,256]{0,1:T(8,128)(2,1)}), bf16[8192,256]{0,1:T(8,128)(2,1)}) %all-gather.20.cloned.1.call-update) | async-done | bytes 4194320 | tf_op jit(solution)/shard_map/all_gather | solution.py:54
  753.1 4.0 copy.33
  760.9 18.6 %all-gather.6 = bf16[512,256]{1,0:T(8,128)(2,1)S(1)} all-gather(bf16[32,256]{1,0:T(8,128)(2,1)S(1)} %fusion.14), channel_id=8, replica_groups=mesh['leaf'=16,'row'=16] {'leaf'}, dimensions={0}, use_global_device_ids=true | all-gather | bytes 278528 | tf_op jit(solution)/shard_map/all_gather | solution.py:47
  781.8 44.1 %all-gather.22.cloned.1.call-done = bf16[8192,256]{0,1:T(8,128)(2,1)} async-done(((bf16[512,256]{0,1:T(8,128)(2,1)}), bf16[8192,256]{0,1:T(8,128)(2,1)}) %all-gather.22.cloned.1.call-update) | async-done | bytes 4194320 | tf_op jit(solution)/shard_map/all_gather | solution.py:54
  825.9 4.0 copy.34
  830.0 2.5 bitcast_reduce_fusion.1
  833.7 18.8 %all-gather.8 = bf16[512,256]{1,0:T(8,128)(2,1)S(1)} all-gather(bf16[32,256]{1,0:T(8,128)(2,1)S(1)} %fusion.15), channel_id=10, replica_groups=mesh['leaf'=16,'row'=16] {'leaf'}, dimensions={0}, use_global_device_ids=true | all-gather | bytes 278528 | tf_op jit(solution)/shard_map/all_gather | solution.py:47
  857.5 41.5 %all-gather.24.cloned.1.call-done = bf16[8192,256]{0,1:T(8,128)(2,1)} async-done(((bf16[512,256]{0,1:T(8,128)(2,1)}), bf16[8192,256]{0,1:T(8,128)(2,1)}) %all-gather.24.cloned.1.call-update) | async-done | bytes 4194320 | tf_op jit(solution)/shard_map/all_gather | solution.py:54
  899.1 4.0 copy.35
  (202 shorter events, 81.5 us)
Async XLA Ops:
  7.2 102.7 %reduce-scatter.16.cloned.1.call-start = ((), (), s32[]{:S(2)}) async-start(), calls=%async_computation.10 | async-start | bytes 278528
  8.1 101.8 %copy-start.30 = (f32[32]{0:T(128)}, f32[32]{0:T(128)S(1)}, u32[]{:S(2)}) copy-start(f32[32]{0:T(128)S(1)} %get-tuple-element.24) | copy-start | bytes 388
  8.1 205.8 %copy-start.32 = (f32[32]{0:T(128)}, f32[32]{0:T(128)S(1)}, u32[]{:S(2)}) copy-start(f32[32]{0:T(128)S(1)} %get-tuple-element.23) | copy-start | bytes 388
  8.1 309.8 %copy-start.34 = (f32[32]{0:T(128)}, f32[32]{0:T(128)S(1)}, u32[]{:S(2)}) copy-start(f32[32]{0:T(128)S(1)} %get-tuple-element.22) | copy-start | bytes 388
  32.5 603.1 %copy-start.39 = (bf16[1,178]{1,0:T(2,128)(2,1)}, bf16[1,178]{1,0:T(2,128)(2,1)S(1)}, u32[]{:S(2)}) copy-start(bf16[1,178]{1,0:T(2,128)(2,1)S(1)} %get-tuple-element.26) | copy-start | bytes 1072
  36.6 73.2 %copy-start.29 = (bf16[6,1,32,256]{3,2,1,0:T(8,128)(2,1)S(1)}, bf16[6,1,32,256]{3,2,1,0:T(8,128)(2,1)}, u32[]{:S(2)}) copy-start(bf16[6,1,32,256]{3,2,1,0:T(8,128)(2,1)} %param.5) | copy-start | bytes 294916
  36.6 177.2 %reduce-scatter.18.cloned.1.call-start = ((), (), s32[]{:S(2)}) async-start(), calls=%async_computation.11 | async-start | bytes 278528
  142.0 175.9 %reduce-scatter.20.cloned.1.call-start = ((), (), s32[]{:S(2)}) async-start(), calls=%async_computation.12 | async-start | bytes 278528
  213.8 23.3 %copy-start.2 = (bf16[1,40,32,512]{3,2,1,0:T(8,128)(2,1)S(1)}, bf16[1,40,32,512]{3,2,1,0:T(8,128)(2,1)}, u32[]{:S(2)}) copy-start(bf16[1,40,32,512]{3,2,1,0:T(8,128)(2,1)} %slice.238) | copy-start | bytes 3932164
  246.0 175.5 %reduce-scatter.22.cloned.1.call-start = ((), (), s32[]{:S(2)}) async-start(), calls=%async_computation.13 | async-start | bytes 278528
  317.8 23.2 %copy-start.7 = (bf16[1,32,32,512]{3,2,1,0:T(8,128)(2,1)S(1)}, bf16[1,32,32,512]{3,2,1,0:T(8,128)(2,1)}, u32[]{:S(2)}) copy-start(bf16[1,32,32,512]{3,2,1,0:T(8,128)(2,1)} %slice.249) | copy-start | bytes 3145732
  349.7 172.7 %reduce-scatter.24.cloned.1.call-start = ((), (), s32[]{:S(2)}) async-start(), calls=%async_computation.14 | async-start | bytes 278528
  350.8 97.1 %copy-start.5 = (bf16[1,16,32,512]{3,2,1,0:T(8,128)(2,1)}, bf16[1,16,32,512]{3,2,1,0:T(8,128)(2,1)S(1)}, u32[]{:S(2)}) copy-start(bf16[1,16,32,512]{3,2,1,0:T(8,128)(2,1)S(1)} %slice.261) | copy-start | bytes 1572868
  450.5 157.3 %all-gather.16.cloned.1.call-start = ((), (), s32[]{:S(2)}) async-start(), calls=%async_computation.5 | async-start | bytes 4456448 | tf_op jit(solution)/shard_map/all_gather | solution.py:54
  522.4 40.8 %copy-start.6 = (bf16[1,16,32,512]{3,2,1,0:T(8,128)(2,1)S(1)}, bf16[1,16,32,512]{3,2,1,0:T(8,128)(2,1)}, u32[]{:S(2)}) copy-start(bf16[1,16,32,512]{3,2,1,0:T(8,128)(2,1)} %copy-done.5) | copy-start | bytes 1572868
  544.9 18.2 %copy-start.28 = (bf16[256,512]{1,0:T(8,128)(2,1)}, bf16[256,512]{1,0:T(8,128)(2,1)S(1)}, u32[]{:S(2)}) copy-start(bf16[256,512]{1,0:T(8,128)(2,1)S(1)} %fusion.5) | copy-start | bytes 786436
  564.2 115.5 %all-gather.18.cloned.1.call-start = ((), (), s32[]{:S(2)}) async-start(), calls=%async_computation.6 | async-start | bytes 4456448 | tf_op jit(solution)/shard_map/all_gather | solution.py:54
  614.3 19.9 %copy-start.8 = (bf16[1,32,32,512]{3,2,1,0:T(8,128)(2,1)S(1)}, bf16[1,32,32,512]{3,2,1,0:T(8,128)(2,1)}, u32[]{:S(2)}) copy-start(bf16[1,32,32,512]{3,2,1,0:T(8,128)(2,1)} %slice.249) | copy-start | bytes 3145732
  635.5 117.7 %all-gather.20.cloned.1.call-start = ((), (), s32[]{:S(2)}) async-start(), calls=%async_computation.7 | async-start | bytes 4456448 | tf_op jit(solution)/shard_map/all_gather | solution.py:54
  683.7 2.6 copy-start.15
  683.7 2.6 copy-start.35
  686.3 21.4 %copy-start.3 = (bf16[1,40,32,512]{3,2,1,0:T(8,128)(2,1)S(1)}, bf16[1,40,32,512]{3,2,1,0:T(8,128)(2,1)}, u32[]{:S(2)}) copy-start(bf16[1,40,32,512]{3,2,1,0:T(8,128)(2,1)} %slice.238) | copy-start | bytes 3932164
  708.9 117.0 %all-gather.22.cloned.1.call-start = ((), (), s32[]{:S(2)}) async-start(), calls=%async_computation.8 | async-start | bytes 4456448 | tf_op jit(solution)/shard_map/all_gather | solution.py:54
  757.2 2.6 copy-start.19
  757.2 2.6 copy-start.33
  757.2 23.0 %copy-start.21 = (bf16[8,32,256]{2,1,0:T(8,128)(2,1)S(1)}, bf16[8,32,256]{2,1,0:T(8,128)(2,1)}, u32[]{:S(2)}) copy-start(bf16[8,32,256]{2,1,0:T(8,128)(2,1)} %copy-done.20) | copy-start | bytes 393220
  757.2 23.0 %copy-start.42 = (bf16[44]{0:T(256)(128)(2,1)S(1)}, bf16[44]{0:T(256)(128)(2,1)}, u32[]{:S(2)}) copy-start(bf16[44]{0:T(256)(128)(2,1)} %slice_bitcast_fusion.1) | copy-start | bytes 268
  781.7 117.4 %all-gather.24.cloned.1.call-start = ((), (), s32[]{:S(2)}) async-start(), calls=%async_computation.9 | async-start | bytes 4456448 | tf_op jit(solution)/shard_map/all_gather | solution.py:54
  829.9 2.6 copy-start.13
  830.0 2.6 copy-start.31
  830.0 23.4 %copy-start.23 = (bf16[512,256]{1,0:T(8,128)(2,1)S(1)}, bf16[512,256]{1,0:T(8,128)(2,1)}, u32[]{:S(2)}) copy-start(bf16[512,256]{1,0:T(8,128)(2,1)} %copy-done.22) | copy-start | bytes 786436
  857.5 45.6 %copy-start.36 = (bf16[6,32,256]{2,1,0:T(8,128)(2,1)}, bf16[6,32,256]{2,1,0:T(8,128)(2,1)S(1)}, u32[]{:S(2)}) copy-start(bf16[6,32,256]{2,1,0:T(8,128)(2,1)S(1)} %constant_dynamic-update-slice_fusion) | copy-start | bytes 294916
  (21 other events, 21.1 us)
Sparse Core Ops, SparseCore 0:
  36.7 73.0 reduce-scatter.15
  142.1 71.6 reduce-scatter.17
  246.1 71.6 reduce-scatter.19
  349.8 71.6 reduce-scatter.21
  450.6 71.6 reduce-scatter.23
  564.3 43.3 all-gather.15
  635.6 44.0 all-gather.17
  709.1 44.0 all-gather.19
  781.8 44.0 all-gather.21
  855.0 44.0 all-gather.23
